TPU v7x, 1024 devices: a whole 4x4x32 slice. The times are simulated.
1024 devices in a mesh: dp: 64 (over z, core), et: 16 (over y, x).
Axes of the slice: x: 4, y: 4, z: 32, core: 2. Of those that a mesh axis runs over, the one named last changes fastest.
Arguments:
- pre_gate: bfloat16 [16384, 5376], P('dp', 'et'), may hold values from -6 to 6
- pre_up: bfloat16 [16384, 5376], P('dp', 'et'), may hold values from -6 to 6
- down_weight: bfloat16 [5376, 6144], P('et'), may hold values from -0.078125 to 0.078125
- row_token: int32 [16384], P('dp'), may hold values from 0 to 384, as said below
- block_count: int32 [64], P('dp'), may hold values from 1 to 2, as said below
- router_logits: float32 [24576, 16], P('dp'), as said below
- tokens_in: bfloat16 [24576, 6144], P('dp', 'et'), may hold values from -6 to 6
- out_grad: bfloat16 [24576, 6144], P('dp', 'et'), may hold values from -12 to 12
Outputs:
- combined: bfloat16 [24576, 6144], P('dp', 'et')
- grad_gate: bfloat16 [16384, 5376], P('dp', 'et')
- grad_up: bfloat16 [16384, 5376], P('dp', 'et')
- router_grad: float32 [16, 6144], P(None, 'et')
Inputs may be any that keep to these rules, and one draw needn't show every extreme that they name: `row_token`: within the 256 slots of one index of dp, the first r slots hold distinct tokens below 384 and the other slots hold 384, with r between 64 and 256; r = 256 on at least one index of dp. `block_count`: the number of blocks of 128 slots that hold r's live slots, rounded up, on each index of dp. `router_logits`: finite router scores.
All inputs are finite; a program needn't handle non-finite values.
Results may differ from a plain program's by a relative error of at most 0.0051.
Values may be sent and summed in bfloat16 or wider, within the bound.
A program may use at most 64 MiB of HBM per device.

v0:
```python
import jax
import jax.numpy as jnp
from jax import lax
from jax.sharding import PartitionSpec as P

BLOCK = 128


def body(pre_gate, pre_up, down_weight, row_token, block_count, router_logits, tokens_in, out_grad):
    slot_count = pre_gate.shape[0]
    tok_count = tokens_in.shape[0]
    slot_ids = jnp.arange(slot_count, dtype=jnp.int32)
    live_slot = (slot_ids // BLOCK < block_count[0]) & (row_token < tok_count)
    scatter_index = jnp.where(live_slot, row_token, tok_count)
    safe_index = jnp.minimum(scatter_index, tok_count - 1)
    router_probs = jax.nn.softmax(router_logits, axis=-1)
    first_prob = router_probs[:, 0]
    row_prob = jnp.where(live_slot, first_prob[safe_index], 0.0)
    gate_value = pre_gate.astype(jnp.float32)
    up_value = pre_up.astype(jnp.float32)
    sigmoid_gate = jax.nn.sigmoid(gate_value)
    hidden = jnp.where(live_slot[:, None], gate_value * sigmoid_gate * up_value, 0.0).astype(
        jnp.bfloat16
    )
    partial_out = jnp.dot(hidden, down_weight, preferred_element_type=jnp.float32)
    expert_out = lax.psum_scatter(partial_out, "et", scatter_dimension=1, tiled=True)
    combined = (
        jnp.zeros((tok_count, expert_out.shape[1]), jnp.float32)
        .at[scatter_index]
        .add(row_prob[:, None] * expert_out, mode="drop")
        .astype(jnp.bfloat16)
    )
    local_rows = jnp.where(live_slot[:, None], out_grad[safe_index], 0.0)
    dot_part = jnp.sum(local_rows.astype(jnp.float32) * expert_out, axis=1)
    weight_grad = lax.psum(dot_part, "et")
    gathered = lax.all_gather(out_grad, "et", axis=1, tiled=True)
    slot_rows = jnp.where(live_slot[:, None], gathered[safe_index], 0.0)
    raw_back = lax.dot_general(
        slot_rows, down_weight, (((1,), (1,)), ((), ())), preferred_element_type=jnp.float32
    )
    hidden_grad = row_prob[:, None] * raw_back
    grad_up = (hidden_grad * gate_value * sigmoid_gate).astype(jnp.bfloat16)
    grad_gate = (
        hidden_grad * up_value * sigmoid_gate * (1.0 + gate_value * (1.0 - sigmoid_gate))
    ).astype(jnp.bfloat16)
    token_weight = (
        jnp.zeros((tok_count,), jnp.float32).at[scatter_index].add(weight_grad, mode="drop")
    )
    one_hot = (jnp.arange(router_probs.shape[1]) == 0).astype(jnp.float32)
    logit_grad = (
        first_prob[:, None] * (one_hot[None, :] - router_probs) * token_weight[:, None]
    ).astype(jnp.bfloat16)
    router_part = jnp.dot(logit_grad.T, tokens_in, preferred_element_type=jnp.float32)
    all_tokens = tok_count * lax.axis_size("dp")
    router_grad = lax.psum(router_part, "dp") * all_tokens ** (-0.5)
    return (combined, grad_gate, grad_up, router_grad)


def solution(mesh):
    in_specs = (
        P("dp", "et"),
        P("dp", "et"),
        P("et", None),
        P("dp"),
        P("dp"),
        P("dp", None),
        P("dp", "et"),
        P("dp", "et"),
    )
    out_specs = (P("dp", "et"), P("dp", "et"), P("dp", "et"), P(None, "et"))
    return jax.shard_map(body, mesh=mesh, in_specs=in_specs, out_specs=out_specs, check_vma=False)
```

profile of v0, /device:TPU:1, one launch (start us, length us, event | category | flops | bytes accessed | tf_op | source)
XLA Modules:
  0.0 470.2 jit_solution(5112984317836175932)
XLA Ops:
  7.2 0.0 copy-start
  7.2 0.0 all-gather.2.cloned.1.call-start
  7.2 0.7 all-gather.2.cloned.1.call-update
  7.9 0.0 reduce-scatter.2.cloned.1.call-start
  8.6 0.7 compare_select_fusion
  9.3 6.9 %fusion.22 = f32[256,6144]{1,0:T(8,128)} fusion(bf16[336,6144]{1,0:T(8,128)(2,1)} %param.10, bf16[256,336]{0,1:T(8,128)(2,1)} %param.9, bf16[256,336]{0,1:T(8,128)(2,1)} %param.8, pred[256]{0:T(512)(128)(4,1)S(1)} %get-tuple-element.5), kind=kOutput, calls=%fused_computation.32 | convolution fusion | flops 1057738752 | bytes 10764544 | tf_op jit(solution)/shard_map/dot_general | solution.py:25
  16.2 0.0 copy-start.1
  16.2 0.0 copy-start.2
  16.2 0.0 copy-start.3
  16.2 0.0 reduce-scatter.2.cloned.1.call-update
  16.2 0.9 copy-done.1
  17.2 1.8 gather_fusion.2
  19.0 0.0 copy-done.2
  19.1 1.9 gather_fusion
  21.0 0.0 copy-done.3
  21.1 94.5 %all-gather.2.cloned.1.call-done = bf16[384,6144]{1,0:T(8,128)(2,1)} async-done(((bf16[384,384]{1,0:T(8,128)(2,1)}), bf16[384,6144]{1,0:T(8,128)(2,1)}) %all-gather.2.cloned.1.call-update) | async-done | bytes 4718608 | tf_op jit(solution)/shard_map/all_gather | solution.py:36
  115.6 8.4 %gather_fusion.1 = bf16[256,6144]{1,0:T(8,128)(2,1)S(1)} fusion(bf16[384,6144]{1,0:T(8,128)(2,1)} %all-gather.2.cloned.1.call-done, s32[1024]{0:T(1024)S(1)} %pad_clamp_fusion), kind=kCustom, calls=%fused_computation.1 | custom fusion | bytes 6292480 | tf_op jit(solution)/shard_map/gather | solution.py:37
  124.0 4.4 fusion.19
  128.4 109.3 %reduce-scatter.2.cloned.1.call-done = f32[256,384]{1,0:T(8,128)} async-done(((f32[256,6144]{1,0:T(8,128)}), f32[256,384]{1,0:T(8,128)}) %reduce-scatter.2.cloned.1.call-update) | async-done | bytes 393232 | tf_op jit(solution)/shard_map/reduce_scatter | solution.py:26
  237.7 1.2 multiply_reduce_fusion
  239.0 31.0 %psum.14 = f32[256]{0:T(256)S(1)} all-reduce(f32[256]{0:T(256)S(1)} %multiply_reduce_fusion), channel_id=1, replica_groups=mesh['dp'=64,'et'=16] {'et'}, use_global_device_ids=true, to_apply=%region_5.6 | all-reduce | flops 256 | bytes 2048 | tf_op jit(solution)/shard_map/psum | solution.py:35
  270.0 2.3 scatter_custom_fusion.1
  272.3 0.0 copy-done
  272.3 0.2 fusion.29
  272.5 186.7 %psum.15 = f32[16,384]{1,0:T(8,128)S(1)} all-reduce(f32[16,384]{1,0:T(8,128)S(1)} %fusion.29), channel_id=1, replica_groups=mesh['dp'=64,'et'=16] {'dp'}, use_global_device_ids=true, to_apply=%region_7.8 | all-reduce | flops 6144 | bytes 49152 | tf_op jit(solution)/shard_map/psum | solution.py:55
  459.2 0.6 broadcast_multiply_fusion
  459.8 2.8 scatter_custom_fusion
  462.6 0.7 convert_element_type.38
  (8 shorter events, 0.1 us)
Async XLA Ops:
  7.2 265.1 %copy-start = (bf16[384,384]{1,0:T(8,128)(2,1)S(1)}, bf16[384,384]{1,0:T(8,128)(2,1)}, u32[]{:S(2)}) copy-start(bf16[384,384]{1,0:T(8,128)(2,1)} %param.14) | copy-start | bytes 884740
  7.2 108.4 %all-gather.2.cloned.1.call-start = ((), (), s32[]{:S(2)}) async-start(), calls=%async_computation.2 | async-start | bytes 5013504 | tf_op jit(solution)/shard_map/all_gather | solution.py:36
  7.9 229.8 %reduce-scatter.2.cloned.1.call-start = ((), (), s32[]{:S(2)}) async-start(), calls=%async_computation.1 | async-start | bytes 6684672 | tf_op jit(solution)/shard_map/reduce_scatter | solution.py:26
  16.2 1.0 copy-start.1
  16.2 2.8 copy-start.2
  16.2 4.8 %copy-start.3 = (s32[256]{0:T(256)S(1)}, s32[256]{0:T(256)}, u32[]{:S(2)}) copy-start(s32[256]{0:T(256)} %param.11) | copy-start | bytes 3076
Sparse Core Ops, SparseCore 0:
  12.2 103.4 all-gather.1
  121.1 116.6 reduce-scatter.1
where the time goes:
time: 470 us
  blocking collectives  218 us (46%)
  waiting for transfers between devices  205 us (44%)
  between operations  14.8 us (3%)
  local copies, waits for them, and re-layouts  13.1 us (3%)
  matrix products  11.5 us (2%)
  other arithmetic  8.47 us (2%)
    psum x1, blocking collectives, body(): router_grad = lax.psum(router_part, 'dp') * all_tokens ** (-0.5)  187 us
    reduce_scatter x1, waiting for transfers between devices, body(): lax.psum_scatter(partial_out, 'et', scatter_dimension=1, tiled=True)  109 us
    all_gather x1, waiting for transfers between devices, body(): gathered = lax.all_gather(out_grad, 'et', axis=1, tiled=True)  94.5 us
    psum x1, blocking collectives, body(): weight_grad = lax.psum(dot_part, 'et')  31 us
  transfers between devices with their start and end apart: 2, of which 2 were waited for; matrix products, arithmetic and copies ran while one was open for 5% of the time, Pallas kernels for 0%

commit v1 on v0

v1 whole, which is shorter than its diff:
```python
import functools

import jax
import jax.numpy as jnp
from jax import lax
from jax.experimental import pallas as pl
from jax.experimental.pallas import tpu as pltpu
from jax.sharding import PartitionSpec as P

BLOCK = 128
MESH = pl.DeviceIdType.MESH
RING = (1, 3, 2)
F32 = jnp.float32
BF16 = jnp.bfloat16


def kernel(
    nz,
    scale,
    rt_ref,
    bc_ref,
    lg_ref,
    g_ref,
    u_ref,
    w_hbm,
    t_ref,
    og_ref,
    comb_ref,
    gg_ref,
    gu_ref,
    rg_ref,
    wv,
    hid,
    lp,
    onehot,
    pm,
    ct,
    tslot,
    sg,
    raw,
    part,
    r1,
    p2,
    r2,
    wgb,
    rp,
    nearb,
    farb,
    rgb,
    w_sem,
    ag_ss,
    ag_rs,
    r1_ss,
    r1_rs,
    r2_ss,
    r2_rs,
    wg_ss,
    wg_rs,
    near_ss,
    near_rs,
    far_ss,
    far_rs,
    core_ss,
    core_rs,
):
    slots = g_ref.shape[0]
    half = slots // 2
    ff = g_ref.shape[1]
    ffp = hid.shape[1]
    toks, cols = og_ref.shape
    ngrp = nz // 2
    dp = lax.axis_index("dp")
    et = lax.axis_index("et")
    x, y, z, c = et % 4, et // 4, dp // 2, dp % 2
    zp, grp = z % 2, z // 2

    def et_at(yy, xx):
        return (yy % 4) * 4 + xx % 4

    def copy(src, dst, ss, rs, d_dp, d_et):
        return pltpu.make_async_remote_copy(
            src_ref=src, dst_ref=dst, send_sem=ss, recv_sem=rs, device_id=(d_dp, d_et), device_id_type=MESH
        )

    def arrived(ref, rs):
        copy(ref, ref, rs, rs, dp, et_at(y, x + 1)).wait_recv()

    def near_peer(k):
        return (grp * 2 + (zp + k // 2) % 2) * 2 + (c + k) % 2

    barrier = pltpu.get_barrier_semaphore()

    def greet(d_dp, d_et):
        pl.semaphore_signal(barrier, 1, device_id=(d_dp, d_et), device_id_type=MESH)

    def greet_far(k, carry):
        greet((((grp + k) % ngrp) * 2 + zp) * 2 + c, et)
        return carry

    def greet_et(k, carry):
        greet(dp, et_at(y + k // 4, x + k % 4))
        return carry

    lax.fori_loop(1, ngrp, greet_far, 0)
    lax.fori_loop(1, 16, greet_et, 0)
    for k in (1, 2, 3):
        greet(near_peer(k), et)

    w_copy = pltpu.make_async_copy(w_hbm, wv.at[pl.ds(0, ff)], w_sem)
    w_copy.start()

    row_tok = rt_ref[...]
    slot_block = lax.broadcasted_iota(jnp.int32, row_tok.shape, 1) // BLOCK
    row_tok = jnp.where((slot_block < bc_ref[0]) & (row_tok < toks), row_tok, toks).astype(F32)
    row_tok = jnp.broadcast_to(row_tok, (128, slots)).T
    for k in range(toks // 128):
        lane = lax.broadcasted_iota(jnp.int32, (slots, 128), 1).astype(F32) + float(k * 128)
        onehot[:, k * 128 : (k + 1) * 128] = jnp.where(row_tok == lane, 1.0, 0.0).astype(BF16)
    sg[et] = jnp.dot(onehot[...], og_ref[...], preferred_element_type=F32).astype(BF16)

    pl.semaphore_wait(barrier, ngrp - 1 + 15 + 3)

    sends = []

    def send(block, h, d_et):
        view = sg.at[block, pl.ds(h * half, half)]
        cp = copy(view, view, ag_ss.at[len(sends)], ag_rs.at[block * 2 + h], dp, d_et)
        cp.start()
        sends.append(cp)

    def wait_block(block, h):
        arrived(sg.at[block, pl.ds(h * half, half)], ag_rs.at[block * 2 + h])

    for d in RING:
        send(et, 0, et_at(y, x + d))
        send(et, 1, et_at(y + d, x))
    for d in RING:
        send(et, 0, et_at(y + d, x))
        send(et, 1, et_at(y, x + d))

    gate = g_ref[...].astype(F32)
    hid[:, ffp - 128 : ffp] = jnp.zeros((slots, 128), BF16)
    hid[:, 0:ff] = (gate * jax.nn.sigmoid(gate) * u_ref[...].astype(F32)).astype(BF16)
    wv[ff:ffp] = jnp.zeros((ffp - ff, wv.shape[1]), BF16)
    w_copy.wait()
    live_rows = row_tok < float(toks)

    hid[...] = jnp.where(jnp.concatenate([live_rows] * (ffp // 128), axis=1), hid[...], jnp.zeros((), BF16))

    def forward_block(j, carry):
        w_j = wv[:, pl.ds(pl.multiple_of(j * cols, 128), cols)]
        part[j] = jnp.dot(hid[...], w_j, preferred_element_type=F32).astype(BF16)
        return carry

    lax.fori_loop(0, 16, forward_block, 0)

    for d in RING:
        block = et_at(y, x + d)
        wait_block(block, 0)
        for e in RING:
            send(block, 0, et_at(y + e, x))
        block = et_at(y + d, x)
        wait_block(block, 1)
        for e in RING:
            send(block, 1, et_at(y, x + e))

    lp[...] = jnp.zeros(lp.shape, F32)
    lp[:, 0 : lg_ref.shape[1]] = lg_ref[...]
    lane = lax.broadcasted_iota(jnp.int32, lp.shape, 1)
    valid = lane < lg_ref.shape[1]
    logit = lp[...]
    top = jnp.max(jnp.where(valid, logit, -jnp.inf), axis=1, keepdims=True)
    ex = jnp.where(valid, jnp.exp(jnp.where(valid, logit - top, 0.0)), 0.0)
    probs = ex / jnp.sum(ex, axis=1, keepdims=True)
    p0 = probs[:, 0:1]
    coef = p0 * (jnp.where(lane == 0, 1.0, 0.0) - probs)
    table = jnp.where(valid, coef, jnp.where(lane == lg_ref.shape[1], p0, 0.0))
    hi = table.astype(BF16)
    rest = table - hi.astype(F32)
    mid = rest.astype(BF16)
    low = (rest - mid.astype(F32)).astype(BF16)
    pm[...] = (
        jnp.dot(onehot[...], low, preferred_element_type=F32)
        + jnp.dot(onehot[...], mid, preferred_element_type=F32)
        + jnp.dot(onehot[...], hi, preferred_element_type=F32)
    )
    ct[...] = pm[...].T
    tslot[...] = jnp.dot(onehot[...], t_ref[...], preferred_element_type=F32).astype(BF16)

    def back(block):
        w_j = wv[:, pl.ds(pl.multiple_of(block * cols, 128), cols)]
        return lax.dot_general(sg[block], w_j, (((1,), (1,)), ((), ())), preferred_element_type=F32)

    raw[...] = back(et)
    order = [(0, 1), (1, 0), (0, 3), (3, 0), (0, 2), (2, 0)]
    order += [(1, 1), (1, 3), (3, 1), (3, 3), (1, 2), (2, 1), (3, 2), (2, 3), (2, 2)]
    for dy, dx in order:
        block = et_at(y + dy, x + dx)
        if dx == 0:
            wait_block(block, 0)
        elif dy == 0:
            wait_block(block, 1)
        else:
            wait_block(block, 0)
            wait_block(block, 1)
        raw[...] += back(block)

    prod = hid[...].astype(F32) * raw[...]
    fold = prod[:, 0:128]
    for k in range(1, ffp // 128):
        fold = fold + prod[:, k * 128 : (k + 1) * 128]
    wgb[et] = jnp.sum(fold.T, axis=0, keepdims=True)

    def wg_copy(k):
        return copy(wgb.at[et], wgb.at[et], wg_ss.at[k], wg_rs.at[et], dp, et_at(y + k // 4, x + k % 4))

    def wg_send(k, carry):
        wg_copy(k).start()
        return carry

    lax.fori_loop(1, 16, wg_send, 0)

    first = []
    for far_off in (2, 1, 3, 0):
        for d in RING:
            yy, xx = (y + far_off) % 4, (x + d) % 4
            cp = copy(
                part.at[yy * 4 + xx, pl.ds(0, half)],
                r1.at[0, x, yy],
                r1_ss.at[len(first)],
                r1_rs.at[x * 4 + yy],
                dp,
                et_at(y, xx),
            )
            cp.start()
            first.append(cp)
            yy, xx = (y + d) % 4, (x + far_off) % 4
            cp = copy(
                part.at[yy * 4 + xx, pl.ds(half, half)],
                r1.at[1, y, xx],
                r1_ss.at[len(first)],
                r1_rs.at[16 + y * 4 + xx],
                dp,
                et_at(yy, x),
            )
            cp.start()
            first.append(cp)

    p_col = pm[:, lg_ref.shape[1] : lg_ref.shape[1] + 1]
    gate = g_ref[...].astype(F32)
    sig = jax.nn.sigmoid(gate)
    back_p = p_col * raw[:, 0:ff]
    gu_ref[...] = (back_p * gate * sig).astype(BF16)
    gg_ref[...] = (back_p * u_ref[...].astype(F32) * sig * (1.0 + gate * (1.0 - sig))).astype(BF16)

    def wg_wait(k, carry):
        src = et_at(y + k // 4, x + k % 4)
        arrived(wgb.at[src], wg_rs.at[src])
        return carry

    lax.fori_loop(1, 16, wg_wait, 0)
    wg = wgb[0]
    for k in range(1, 16):
        wg = wg + wgb[k]

    lgrad = (ct[0:16] * wg).astype(BF16)
    rpart = jnp.dot(lgrad, tslot[...], preferred_element_type=F32)
    rp[0] = rpart[0:8]
    rp[1] = rpart[8:16]
    mine = zp * 2 + c
    nears = []
    for k in (1, 2, 3):
        cp = copy(
            rp.at[(c + k) % 2], nearb.at[mine], near_ss.at[k], near_rs.at[mine], near_peer(k), et
        )
        cp.start()
        nears.append(cp)
    nearb[mine] = rp[c]
    for k in (1, 2, 3):
        src = ((zp + k // 2) % 2) * 2 + (c + k) % 2
        arrived(nearb.at[src], near_rs.at[src])
    total = ((nearb[0] + nearb[1]) + nearb[2]) + nearb[3]

    pieces = [total[:, k * 128 : (k + 1) * 128] for k in range(cols // 128)]
    pad = farb.shape[1] - 8 * len(pieces)
    farb[grp] = jnp.concatenate(pieces + [jnp.zeros((pad, 128), F32)], axis=0).astype(BF16)

    def far_copy(k):
        to = (((grp + k) % ngrp) * 2 + zp) * 2 + c
        return copy(farb.at[grp], farb.at[grp], far_ss.at[k], far_rs.at[grp], to, et)

    def far_send(i, carry):
        k = ngrp // 2 + (1 - 2 * (i % 2)) * ((i + 1) // 2)
        far_copy(k).start()
        return carry

    lax.fori_loop(0, ngrp - 1, far_send, 0)

    def row_sum(h, k):
        own = part[k * 4 + x, 0:half] if h == 0 else part[y * 4 + k, half:slots]
        acc = own.astype(F32)
        here = x if h == 0 else y
        for d in RING:
            src = (here + d) % 4
            arrived(r1.at[h, src, k], r1_rs.at[h * 16 + src * 4 + k])
            acc = acc + r1[h, src, k].astype(F32)
        return acc

    second = []
    for d in (2, 1, 3):
        for h in (0, 1):
            here = y if h == 0 else x
            k = (here + d) % 4
            p2[h, d] = row_sum(h, k).astype(BF16)
            to = et_at(k, x) if h == 0 else et_at(y, k)
            cp = copy(p2.at[h, d], r2.at[h, here], r2_ss.at[h * 4 + d], r2_rs.at[h * 4 + here], dp, to)
            cp.start()
            second.append(cp)

    def far_wait(k, carry):
        src = (grp + k) % ngrp
        arrived(farb.at[src], far_rs.at[src])
        return carry

    lax.fori_loop(1, ngrp, far_wait, 0)

    def far_add(k, acc):
        return acc + farb[k].astype(F32)

    total = lax.fori_loop(1, ngrp, far_add, farb[0].astype(F32)) * scale
    rgb[c] = jnp.concatenate([total[k * 8 : (k + 1) * 8] for k in range(cols // 128)], axis=1)
    swap = copy(rgb.at[c], rgb.at[c], core_ss, core_rs, near_peer(1), et)
    swap.start()

    out_rows = []
    for h in (0, 1):
        here = y if h == 0 else x
        acc = row_sum(h, here)
        for d in RING:
            src = (here + d) % 4
            arrived(r2.at[h, src], r2_rs.at[h * 4 + src])
            acc = acc + r2[h, src].astype(F32)
        out_rows.append(
            (acc * pm[h * half : (h + 1) * half, lg_ref.shape[1] : lg_ref.shape[1] + 1]).astype(BF16)
        )
    comb_ref[...] = lax.dot_general(
        onehot[...], jnp.concatenate(out_rows, axis=0), (((0,), (0,)), ((), ())), preferred_element_type=F32
    ).astype(BF16)

    arrived(rgb.at[1 - c], core_rs)
    rg_ref[0:8] = rgb[0]
    rg_ref[8:16] = rgb[1]

    for cp in sends + first + second + nears:
        cp.wait_send()

    def wg_done(k, carry):
        wg_copy(k).wait_send()
        return carry

    def far_done(k, carry):
        far_copy(k).wait_send()
        return carry

    lax.fori_loop(1, 16, wg_done, 0)
    lax.fori_loop(1, ngrp, far_done, 0)
    swap.wait_send()


def body(nz, pre_gate, pre_up, down_weight, row_token, block_count, router_logits, tokens_in, out_grad):
    slots, ff = pre_gate.shape
    toks, cols = tokens_in.shape
    half = slots // 2
    ffp = -(-ff // 128) * 128
    wide = down_weight.shape[1]
    ngrp = nz // 2
    experts = router_logits.shape[1]
    far_rows = -(-(8 * (cols // 128)) // 16) * 16
    scale = float((toks * nz * 2) ** -0.5)
    vmem = pl.BlockSpec(memory_space=pltpu.VMEM)
    dma = pltpu.SemaphoreType.DMA
    return pl.pallas_call(
        functools.partial(kernel, nz, scale),
        out_shape=(
            jax.ShapeDtypeStruct((toks, cols), BF16),
            jax.ShapeDtypeStruct((slots, ff), BF16),
            jax.ShapeDtypeStruct((slots, ff), BF16),
            jax.ShapeDtypeStruct((experts, cols), F32),
        ),
        in_specs=[
            vmem,
            pl.BlockSpec(memory_space=pltpu.SMEM),
            vmem,
            vmem,
            vmem,
            pl.BlockSpec(memory_space=pl.ANY),
            vmem,
            vmem,
        ],
        out_specs=(vmem, vmem, vmem, vmem),
        scratch_shapes=[
            pltpu.VMEM((ffp, wide), BF16),
            pltpu.VMEM((slots, ffp), BF16),
            pltpu.VMEM((toks, 128), F32),
            pltpu.VMEM((slots, toks), BF16),
            pltpu.VMEM((slots, 128), F32),
            pltpu.VMEM((128, slots), F32),
            pltpu.VMEM((slots, cols), BF16),
            pltpu.VMEM((16, slots, cols), BF16),
            pltpu.VMEM((slots, ffp), F32),
            pltpu.VMEM((16, slots, cols), BF16),
            pltpu.VMEM((2, 4, 4, half, cols), BF16),
            pltpu.VMEM((2, 4, half, cols), BF16),
            pltpu.VMEM((2, 4, half, cols), BF16),
            pltpu.VMEM((16, 1, slots), F32),
            pltpu.VMEM((2, 8, cols), F32),
            pltpu.VMEM((4, 8, cols), F32),
            pltpu.VMEM((ngrp, far_rows, 128), BF16),
            pltpu.VMEM((2, 8, cols), F32),
            dma,
            dma((30,)),
            dma((32,)),
            dma((24,)),
            dma((32,)),
            dma((8,)),
            dma((8,)),
            dma((16,)),
            dma((16,)),
            dma((4,)),
            dma((4,)),
            dma((ngrp,)),
            dma((ngrp,)),
            dma,
            dma,
        ],
        compiler_params=pltpu.CompilerParams(
            collective_id=1, has_side_effects=True, vmem_limit_bytes=48 * 2**20
        ),
        cost_estimate=pl.CostEstimate(
            flops=4 * slots * ff * wide, bytes_accessed=2 * ff * wide, transcendentals=slots * ff
        ),
        name="expert_down",
    )(
        row_token.reshape(1, slots),
        block_count,
        router_logits,
        pre_gate,
        pre_up,
        down_weight,
        tokens_in,
        out_grad,
    )


def solution(mesh):
    in_specs = (
        P("dp", "et"),
        P("dp", "et"),
        P("et", None),
        P("dp"),
        P("dp"),
        P("dp", None),
        P("dp", "et"),
        P("dp", "et"),
    )
    out_specs = (P("dp", "et"), P("dp", "et"), P("dp", "et"), P(None, "et"))
    nz = mesh.shape["dp"] // 2
    return jax.shard_map(
        functools.partial(body, nz), mesh=mesh, in_specs=in_specs, out_specs=out_specs, check_vma=False
    )
```

time: 470 us -> 93.7 us (0.20)
  blocking collectives: 218 us -> 0 us
  waiting for transfers between devices: 205 us -> 0 us
  Pallas kernels: 0 us -> 81.2 us
  between operations: 14.8 us -> 1.31 us
  matrix products: 11.5 us -> 0 us
  other arithmetic: 8.47 us -> 0 us
    psum x2 -> x0, blocking collectives: 218 us -> none  [the longest x1 187 us: body(): router_grad = lax.psum(router_part, 'dp') * all_tokens ** (-0.5)]
    reduce_scatter x1 -> x0, waiting for transfers between devices: 109 us -> none  [body(): lax.psum_scatter(partial_out, 'et', scatter_dimension=1, tiled=True)]
    all_gather x1 -> x0, waiting for transfers between devices: 94.5 us -> none  [body(): gathered = lax.all_gather(out_grad, 'et', axis=1, tiled=True)]
    pallas_call x0 -> x1, Pallas kernels: none -> 81.2 us  [body(): pl.pallas_call(functools.partial(kernel, nz, scale), out_shape=(jax.Shape...]
    gather x3 -> x0, local copies, waits for them, and re-layouts: 12.2 us -> none  [the longest x1 8.41 us: body(): slot_rows = jnp.where(live_slot[:, None], gathered[safe_index], 0.0)]
    dot_general x3 -> x0, matrix products: 11.5 us -> none  [the longest x1 6.9 us: body(): jnp.dot(hidden, down_weight, preferred_element_type=jnp.float32)]
    unnamed x8 -> x13, local copies, waits for them, and re-layouts: 0.94 us -> 9.12 us
    scatter-add x2 -> x0, other arithmetic: 5.1 us -> none  [the longest x1 2.78 us: body(): combined = jnp.zeros((tok_count, expert_out.shape[1]), jnp.float32).at[sc...]
  transfers between devices with their start and end apart: 2 -> 0, of which waited for: 2 -> 0; matrix products, arithmetic and copies ran while one was open for 5% -> 0% of each run, Pallas kernels for 0% -> 0%
where the time goes in v1:
time: 93.7 us; the launch traced here: 93.3 us
  Pallas kernels  81.2 us (87%)
  local copies, waits for them, and re-layouts  10.7 us (11%)
  between operations  1.31 us (1%)
    pallas_call x1, Pallas kernels, body(): pl.pallas_call(functools.partial(kernel, nz, scale), out_shape=(jax.Shape...  81.2 us
    unnamed x13, local copies, waits for them, and re-layouts  9.12 us

profile of v1, /device:TPU:1, one launch (start us, length us, event | category | flops | bytes accessed | tf_op | source)
XLA Modules:
  0.0 93.3 jit_solution(15126375222124625383)
XLA Ops:
  1.3 1.1 %copy.13.g_ref = bf16[256,336]{1,0:T(8,128)(2,1)S(1)} copy(bf16[256,336]{0,1:T(8,128)(2,1)} %param.8) | data formatting | bytes 344064 | tf_op args[0]
  2.4 1.1 %copy.14.u_ref = bf16[256,336]{1,0:T(8,128)(2,1)S(1)} copy(bf16[256,336]{0,1:T(8,128)(2,1)} %param.9) | data formatting | bytes 344064 | tf_op args[1]
  3.4 0.9 copy.12.lg_ref
  4.3 0.0 copy-start
  4.3 2.2 %copy-done = bf16[336,6144]{1,0:T(8,128)(2,1)S(1)} copy-done((bf16[336,6144]{1,0:T(8,128)(2,1)S(1)}, bf16[336,6144]{1,0:T(8,128)(2,1)}, u32[]{:S(2)}) %copy-start) | copy-done | bytes 4128792
  6.5 0.0 copy-start.1
  6.5 1.0 %copy-done.1 = bf16[384,384]{1,0:T(8,128)(2,1)S(1)} copy-done((bf16[384,384]{1,0:T(8,128)(2,1)S(1)}, bf16[384,384]{1,0:T(8,128)(2,1)}, u32[]{:S(2)}) %copy-start.1) | copy-done | bytes 294936
  7.5 0.0 copy-start.2
  7.5 1.0 %copy-done.2 = bf16[384,384]{1,0:T(8,128)(2,1)S(1)} copy-done((bf16[384,384]{1,0:T(8,128)(2,1)S(1)}, bf16[384,384]{1,0:T(8,128)(2,1)}, u32[]{:S(2)}) %copy-start.2) | copy-done | bytes 294936
  8.4 0.0 copy-start.3
  8.4 0.7 copy-done.3
  9.1 81.2 %expert_down.1 = (bf16[384,384]{1,0:T(8,128)(2,1)S(1)}, bf16[256,336]{1,0:T(8,128)(2,1)S(1)}, bf16[256,336]{1,0:T(8,128)(2,1)S(1)}, f32[16,384]{1,0:T(8,128)S(1)}) custom-call(s32[1,256]{1,0:T(1,128)S(1)} %bitcast.1, s32[1]{0:T(128)S(6)} %copy.19.bc_ref, f32[384,16]{1,0:T(8,128)S(1)} %copy.12.lg_ref, bf16[256,336]{1,0:T(8,128)(2,1)S(1)} %copy.13.g_ref, ...), custom_call_target="tpu_custom_call" | custom-call | flops 2113929216 | bytes 4128768 | tf_op jit(solution)/shard_map/expert_down/pallas_call | solution.py:382
  90.3 0.8 copy.15
  91.2 0.8 copy.16
  92.0 0.7 copy.20
  92.7 0.6 copy.21
Async XLA Ops:
  4.3 2.2 %copy-start = (bf16[336,6144]{1,0:T(8,128)(2,1)S(1)}, bf16[336,6144]{1,0:T(8,128)(2,1)}, u32[]{:S(2)}) copy-start(bf16[336,6144]{1,0:T(8,128)(2,1)} %w_hbm.1) | copy-start | bytes 12386308
  6.5 1.0 %copy-start.1 = (bf16[384,384]{1,0:T(8,128)(2,1)S(1)}, bf16[384,384]{1,0:T(8,128)(2,1)}, u32[]{:S(2)}) copy-start(bf16[384,384]{1,0:T(8,128)(2,1)} %t_ref.1) | copy-start | bytes 884740
  7.5 1.0 %copy-start.2 = (bf16[384,384]{1,0:T(8,128)(2,1)S(1)}, bf16[384,384]{1,0:T(8,128)(2,1)}, u32[]{:S(2)}) copy-start(bf16[384,384]{1,0:T(8,128)(2,1)} %og_ref.1) | copy-start | bytes 884740
  8.4 0.7 copy-start.3

commit v2 on v1

--- a/solution.py
+++ b/solution.py
@@ -17,21 +17,27 @@
 def kernel(
     nz,
     scale,
-    rt_ref,
+    rt_hbm,
     bc_ref,
-    lg_ref,
-    g_ref,
-    u_ref,
+    lg_hbm,
+    g_hbm,
+    u_hbm,
     w_hbm,
-    t_ref,
-    og_ref,
+    t_hbm,
+    og_hbm,
     comb_ref,
     gg_ref,
     gu_ref,
     rg_ref,
+    rt,
+    lg,
+    gt,
+    ut,
     wv,
+    tv,
+    og,
+    hid_t,
     hid,
-    lp,
     onehot,
     pm,
     ct,
@@ -47,7 +53,8 @@
     nearb,
     farb,
     rgb,
-    w_sem,
+    in_sem,
+    ready,
     ag_ss,
     ag_rs,
     r1_ss,
@@ -63,11 +70,11 @@
     core_ss,
     core_rs,
 ):
-    slots = g_ref.shape[0]
+    ff, slots = gt.shape
     half = slots // 2
-    ff = g_ref.shape[1]
     ffp = hid.shape[1]
-    toks, cols = og_ref.shape
+    toks, cols = og.shape
+    experts = lg.shape[0]
     ngrp = nz // 2
     dp = lax.axis_index("dp")
     et = lax.axis_index("et")
@@ -88,37 +95,55 @@
     def near_peer(k):
         return (grp * 2 + (zp + k // 2) % 2) * 2 + (c + k) % 2
 
+    loads = {}
+    pairs = dict(
+        rt=(rt_hbm, rt), og=(og_hbm, og), g=(g_hbm, gt), u=(u_hbm, ut),
+        w=(w_hbm, wv.at[pl.ds(0, ff)]), lg=(lg_hbm, lg), t=(t_hbm, tv),
+    )
+    for i, (name, (src, dst)) in enumerate(pairs.items()):
+        loads[name] = pltpu.make_async_copy(src, dst, in_sem.at[i])
+        loads[name].start()
+
     barrier = pltpu.get_barrier_semaphore()
 
-    def greet(d_dp, d_et):
-        pl.semaphore_signal(barrier, 1, device_id=(d_dp, d_et), device_id_type=MESH)
-
-    def greet_far(k, carry):
-        greet((((grp + k) % ngrp) * 2 + zp) * 2 + c, et)
-        return carry
+    def greet(sem, d_dp, d_et):
+        pl.semaphore_signal(sem, 1, device_id=(d_dp, d_et), device_id_type=MESH)
 
     def greet_et(k, carry):
-        greet(dp, et_at(y + k // 4, x + k % 4))
-        return carry
-
-    lax.fori_loop(1, ngrp, greet_far, 0)
+        greet(barrier, dp, et_at(y + k // 4, x + k % 4))
+        return carry
+
+    def line(k):
+        return (((grp + ngrp + k) % ngrp) * 2 + zp) * 2 + c
+
+    greet(barrier, line(1), et)
+    greet(barrier, line(-1), et)
     lax.fori_loop(1, 16, greet_et, 0)
     for k in (1, 2, 3):
-        greet(near_peer(k), et)
-
-    w_copy = pltpu.make_async_copy(w_hbm, wv.at[pl.ds(0, ff)], w_sem)
-    w_copy.start()
-
-    row_tok = rt_ref[...]
+        greet(barrier, near_peer(k), et)
+
+    steps = ngrp.bit_length() - 2
+
+    def ready_signal(i):
+        greet(ready.at[i], line(1 << i), et)
+        greet(ready.at[i], line(-(1 << i)), et)
+
+    def ready_wait(i):
+        pl.semaphore_wait(ready.at[i], 2)
+
+    loads["rt"].wait()
+    row_tok = rt[...]
     slot_block = lax.broadcasted_iota(jnp.int32, row_tok.shape, 1) // BLOCK
     row_tok = jnp.where((slot_block < bc_ref[0]) & (row_tok < toks), row_tok, toks).astype(F32)
+    live = row_tok < float(toks)
     row_tok = jnp.broadcast_to(row_tok, (128, slots)).T
     for k in range(toks // 128):
         lane = lax.broadcasted_iota(jnp.int32, (slots, 128), 1).astype(F32) + float(k * 128)
         onehot[:, k * 128 : (k + 1) * 128] = jnp.where(row_tok == lane, 1.0, 0.0).astype(BF16)
-    sg[et] = jnp.dot(onehot[...], og_ref[...], preferred_element_type=F32).astype(BF16)
-
-    pl.semaphore_wait(barrier, ngrp - 1 + 15 + 3)
+    loads["og"].wait()
+    sg[et] = jnp.dot(onehot[...], og[...], preferred_element_type=F32).astype(BF16)
+
+    pl.semaphore_wait(barrier, 2 + 15 + 3)
 
     sends = []
 
@@ -138,14 +163,17 @@
         send(et, 0, et_at(y + d, x))
         send(et, 1, et_at(y, x + d))
 
-    gate = g_ref[...].astype(F32)
-    hid[:, ffp - 128 : ffp] = jnp.zeros((slots, 128), BF16)
-    hid[:, 0:ff] = (gate * jax.nn.sigmoid(gate) * u_ref[...].astype(F32)).astype(BF16)
+    ready_signal(0)
+
+    loads["g"].wait()
+    loads["u"].wait()
+    gate = gt[...].astype(F32)
+    hidden = jnp.where(live, gate * jax.nn.sigmoid(gate) * ut[...].astype(F32), 0.0)
+    hid_t[ff:ffp] = jnp.zeros((ffp - ff, slots), F32)
+    hid_t[0:ff] = hidden
+    hid[...] = hid_t[...].T.astype(BF16)
     wv[ff:ffp] = jnp.zeros((ffp - ff, wv.shape[1]), BF16)
-    w_copy.wait()
-    live_rows = row_tok < float(toks)
-
-    hid[...] = jnp.where(jnp.concatenate([live_rows] * (ffp // 128), axis=1), hid[...], jnp.zeros((), BF16))
+    loads["w"].wait()
 
     def forward_block(j, carry):
         w_j = wv[:, pl.ds(pl.multiple_of(j * cols, 128), cols)]
@@ -153,6 +181,9 @@
         return carry
 
     lax.fori_loop(0, 16, forward_block, 0)
+
+    ready_wait(0)
+    ready_signal(1)
 
     for d in RING:
         block = et_at(y, x + d)
@@ -164,32 +195,33 @@
         for e in RING:
             send(block, 1, et_at(y, x + e))
 
-    lp[...] = jnp.zeros(lp.shape, F32)
-    lp[:, 0 : lg_ref.shape[1]] = lg_ref[...]
-    lane = lax.broadcasted_iota(jnp.int32, lp.shape, 1)
-    valid = lane < lg_ref.shape[1]
-    logit = lp[...]
-    top = jnp.max(jnp.where(valid, logit, -jnp.inf), axis=1, keepdims=True)
-    ex = jnp.where(valid, jnp.exp(jnp.where(valid, logit - top, 0.0)), 0.0)
-    probs = ex / jnp.sum(ex, axis=1, keepdims=True)
-    p0 = probs[:, 0:1]
-    coef = p0 * (jnp.where(lane == 0, 1.0, 0.0) - probs)
-    table = jnp.where(valid, coef, jnp.where(lane == lg_ref.shape[1], p0, 0.0))
+    loads["lg"].wait()
+    logit = lg[...]
+    ex = jnp.exp(logit - jnp.max(logit, axis=0, keepdims=True))
+    probs = ex / jnp.sum(ex, axis=0, keepdims=True)
+    p0 = probs[0:1]
+    first_row = lax.broadcasted_iota(jnp.int32, probs.shape, 0) == 0
+    coef = p0 * (jnp.where(first_row, 1.0, 0.0) - probs)
+    table = jnp.concatenate([coef, jnp.broadcast_to(p0, coef.shape)], axis=0)
     hi = table.astype(BF16)
     rest = table - hi.astype(F32)
     mid = rest.astype(BF16)
     low = (rest - mid.astype(F32)).astype(BF16)
-    pm[...] = (
-        jnp.dot(onehot[...], low, preferred_element_type=F32)
-        + jnp.dot(onehot[...], mid, preferred_element_type=F32)
-        + jnp.dot(onehot[...], hi, preferred_element_type=F32)
-    )
-    ct[...] = pm[...].T
-    tslot[...] = jnp.dot(onehot[...], t_ref[...], preferred_element_type=F32).astype(BF16)
+
+    def to_slots(rows):
+        return lax.dot_general(rows, onehot[...], (((1,), (1,)), ((), ())), preferred_element_type=F32)
+
+    ct[...] = (to_slots(low) + to_slots(mid)) + to_slots(hi)
+    pm[...] = jnp.broadcast_to(ct[experts : experts + 1], (128, slots)).T
+    loads["t"].wait()
+    tslot[...] = jnp.dot(onehot[...], tv[...], preferred_element_type=F32).astype(BF16)
+
+    ready_wait(1)
+    ready_signal(2)
 
     def back(block):
-        w_j = wv[:, pl.ds(pl.multiple_of(block * cols, 128), cols)]
-        return lax.dot_general(sg[block], w_j, (((1,), (1,)), ((), ())), preferred_element_type=F32)
+        w_j = wv[0:ff, pl.ds(pl.multiple_of(block * cols, 128), cols)]
+        return lax.dot_general(w_j, sg[block], (((1,), (1,)), ((), ())), preferred_element_type=F32)
 
     raw[...] = back(et)
     order = [(0, 1), (1, 0), (0, 3), (3, 0), (0, 2), (2, 0)]
@@ -205,11 +237,8 @@
             wait_block(block, 1)
         raw[...] += back(block)
 
-    prod = hid[...].astype(F32) * raw[...]
-    fold = prod[:, 0:128]
-    for k in range(1, ffp // 128):
-        fold = fold + prod[:, k * 128 : (k + 1) * 128]
-    wgb[et] = jnp.sum(fold.T, axis=0, keepdims=True)
+    prod = hid_t[0:ff].astype(BF16).astype(F32) * raw[...]
+    wgb[et] = jnp.sum(prod, axis=0, keepdims=True)
 
     def wg_copy(k):
         return copy(wgb.at[et], wgb.at[et], wg_ss.at[k], wg_rs.at[et], dp, et_at(y + k // 4, x + k % 4))
@@ -246,12 +275,11 @@
             cp.start()
             first.append(cp)
 
-    p_col = pm[:, lg_ref.shape[1] : lg_ref.shape[1] + 1]
-    gate = g_ref[...].astype(F32)
+    gate = gt[...].astype(F32)
     sig = jax.nn.sigmoid(gate)
-    back_p = p_col * raw[:, 0:ff]
+    back_p = ct[experts : experts + 1] * raw[...]
     gu_ref[...] = (back_p * gate * sig).astype(BF16)
-    gg_ref[...] = (back_p * u_ref[...].astype(F32) * sig * (1.0 + gate * (1.0 - sig))).astype(BF16)
+    gg_ref[...] = (back_p * ut[...].astype(F32) * sig * (1.0 + gate * (1.0 - sig))).astype(BF16)
 
     def wg_wait(k, carry):
         src = et_at(y + k // 4, x + k % 4)
@@ -263,7 +291,7 @@
     for k in range(1, 16):
         wg = wg + wgb[k]
 
-    lgrad = (ct[0:16] * wg).astype(BF16)
+    lgrad = (ct[0:experts] * wg).astype(BF16)
     rpart = jnp.dot(lgrad, tslot[...], preferred_element_type=F32)
     rp[0] = rpart[0:8]
     rp[1] = rpart[8:16]
@@ -286,8 +314,12 @@
     farb[grp] = jnp.concatenate(pieces + [jnp.zeros((pad, 128), F32)], axis=0).astype(BF16)
 
     def far_copy(k):
-        to = (((grp + k) % ngrp) * 2 + zp) * 2 + c
-        return copy(farb.at[grp], farb.at[grp], far_ss.at[k], far_rs.at[grp], to, et)
+        return copy(farb.at[grp], farb.at[grp], far_ss.at[k], far_rs.at[grp], line(k), et)
+
+    for i in range(2, steps):
+        ready_wait(i)
+        if i < steps - 1:
+            ready_signal(i + 1)
 
     def far_send(i, carry):
         k = ngrp // 2 + (1 - 2 * (i % 2)) * ((i + 1) // 2)
@@ -341,7 +373,7 @@
             arrived(r2.at[h, src], r2_rs.at[h * 4 + src])
             acc = acc + r2[h, src].astype(F32)
         out_rows.append(
-            (acc * pm[h * half : (h + 1) * half, lg_ref.shape[1] : lg_ref.shape[1] + 1]).astype(BF16)
+            (acc * pm[h * half : (h + 1) * half, 0:1]).astype(BF16)
         )
     comb_ref[...] = lax.dot_general(
         onehot[...], jnp.concatenate(out_rows, axis=0), (((0,), (0,)), ((), ())), preferred_element_type=F32
@@ -365,6 +397,16 @@
     lax.fori_loop(1, 16, wg_done, 0)
     lax.fori_loop(1, ngrp, far_done, 0)
     swap.wait_send()
+
+
+def finish(*refs):
+    n = len(refs) // 2
+    sems = refs[-1]
+    copies = [pltpu.make_async_copy(refs[i], refs[n + i], sems.at[i]) for i in range(n)]
+    for cp in copies:
+        cp.start()
+    for cp in copies:
+        cp.wait()
 
 
 def body(nz, pre_gate, pre_up, down_weight, row_token, block_count, router_logits, tokens_in, out_grad):
@@ -378,36 +420,35 @@
     far_rows = -(-(8 * (cols // 128)) // 16) * 16
     scale = float((toks * nz * 2) ** -0.5)
     vmem = pl.BlockSpec(memory_space=pltpu.VMEM)
+    hbm = pl.BlockSpec(memory_space=pltpu.HBM)
     dma = pltpu.SemaphoreType.DMA
-    return pl.pallas_call(
+    shapes = (
+        jax.ShapeDtypeStruct((toks, cols), BF16),
+        jax.ShapeDtypeStruct((ff, slots), BF16),
+        jax.ShapeDtypeStruct((ff, slots), BF16),
+        jax.ShapeDtypeStruct((experts, cols), F32),
+    )
+    results = pl.pallas_call(
         functools.partial(kernel, nz, scale),
-        out_shape=(
-            jax.ShapeDtypeStruct((toks, cols), BF16),
-            jax.ShapeDtypeStruct((slots, ff), BF16),
-            jax.ShapeDtypeStruct((slots, ff), BF16),
-            jax.ShapeDtypeStruct((experts, cols), F32),
-        ),
-        in_specs=[
-            vmem,
-            pl.BlockSpec(memory_space=pltpu.SMEM),
-            vmem,
-            vmem,
-            vmem,
-            pl.BlockSpec(memory_space=pl.ANY),
-            vmem,
-            vmem,
-        ],
+        out_shape=shapes,
+        in_specs=[hbm, pl.BlockSpec(memory_space=pltpu.SMEM), hbm, hbm, hbm, hbm, hbm, hbm],
         out_specs=(vmem, vmem, vmem, vmem),
         scratch_shapes=[
+            pltpu.VMEM((1, slots), jnp.int32),
+            pltpu.VMEM((experts, toks), F32),
+            pltpu.VMEM((ff, slots), BF16),
+            pltpu.VMEM((ff, slots), BF16),
             pltpu.VMEM((ffp, wide), BF16),
+            pltpu.VMEM((toks, cols), BF16),
+            pltpu.VMEM((toks, cols), BF16),
+            pltpu.VMEM((ffp, slots), F32),
             pltpu.VMEM((slots, ffp), BF16),
-            pltpu.VMEM((toks, 128), F32),
             pltpu.VMEM((slots, toks), BF16),
             pltpu.VMEM((slots, 128), F32),
-            pltpu.VMEM((128, slots), F32),
+            pltpu.VMEM((2 * experts, slots), F32),
             pltpu.VMEM((slots, cols), BF16),
             pltpu.VMEM((16, slots, cols), BF16),
-            pltpu.VMEM((slots, ffp), F32),
+            pltpu.VMEM((ff, slots), F32),
             pltpu.VMEM((16, slots, cols), BF16),
             pltpu.VMEM((2, 4, 4, half, cols), BF16),
             pltpu.VMEM((2, 4, half, cols), BF16),
@@ -417,7 +458,8 @@
             pltpu.VMEM((4, 8, cols), F32),
             pltpu.VMEM((ngrp, far_rows, 128), BF16),
             pltpu.VMEM((2, 8, cols), F32),
-            dma,
+            dma((7,)),
+            pltpu.SemaphoreType.REGULAR((8,)),
             dma((30,)),
             dma((32,)),
             dma((24,)),
@@ -434,7 +476,7 @@
             dma,
         ],
         compiler_params=pltpu.CompilerParams(
-            collective_id=1, has_side_effects=True, vmem_limit_bytes=48 * 2**20
+            collective_id=1, has_side_effects=True, vmem_limit_bytes=62 * 2**20
         ),
         cost_estimate=pl.CostEstimate(
             flops=4 * slots * ff * wide, bytes_accessed=2 * ff * wide, transcendentals=slots * ff
@@ -443,13 +485,23 @@
     )(
         row_token.reshape(1, slots),
         block_count,
-        router_logits,
-        pre_gate,
-        pre_up,
+        router_logits.T,
+        pre_gate.T,
+        pre_up.T,
         down_weight,
         tokens_in,
         out_grad,
     )
+    combined, grad_gate, grad_up, router_grad = pl.pallas_call(
+        finish,
+        out_shape=shapes,
+        in_specs=[hbm] * len(shapes),
+        out_specs=(hbm,) * len(shapes),
+        scratch_shapes=[dma((len(shapes),))],
+        compiler_params=pltpu.CompilerParams(vmem_limit_bytes=62 * 2**20),
+        name="write_results",
+    )(*results)
+    return combined, grad_gate.T, grad_up.T, router_grad
 
 
 def solution(mesh):

time: 93.7 us -> 98.1 us (1.047)
  Pallas kernels: 81.2 us -> 96.1 us
  local copies, waits for them, and re-layouts: 10.7 us -> 0 us
    pallas_call x1 -> x2, Pallas kernels: 81.2 us -> 96.1 us  [the longest x1 74.8 us: body(): pl.pallas_call(functools.partial(kernel, nz, scale), out_shape=shapes, in...]
    unnamed x13 -> x0, local copies, waits for them, and re-layouts: 9.12 us -> none
    pallas_call x2 -> x0, local copies, waits for them, and re-layouts: 1.61 us -> none  [body(): pl.pallas_call(functools.partial(kernel, nz, scale), out_shape=(jax.Shape...]
where the time goes in v2:
time: 98.1 us; the launch traced here: 97.4 us
  Pallas kernels  96.1 us (98%)
  between operations  1.29 us (1%)
    pallas_call x1, Pallas kernels, body(): pl.pallas_call(functools.partial(kernel, nz, scale), out_shape=shapes, in...  74.8 us
    pallas_call x1, Pallas kernels, body(): pl.pallas_call(finish, out_shape=shapes, in_specs=[hbm] * len(shapes), ou...  21.2 us

profile of v2, /device:TPU:1, one launch (start us, length us, event | category | flops | bytes accessed | tf_op | source)
XLA Modules:
  0.0 97.4 jit_solution(14209071098348808157)
XLA Ops:
  1.3 74.8 %expert_down.1 = (bf16[384,384]{1,0:T(8,128)(2,1)}, bf16[336,256]{1,0:T(8,128)(2,1)}, bf16[336,256]{1,0:T(8,128)(2,1)}, f32[16,384]{1,0:T(8,128)}) custom-call(s32[1,256]{1,0:T(1,128)} %bitcast.11, s32[1]{0:T(128)S(6)} %copy.12.bc_ref, f32[16,384]{1,0:T(8,128)} %bitcast.10, bf16[336,256]{1,0:T(8,128)(2,1)} %bitcast.6, bf16[336,256]{1,0:T(8,128)(2,1)} %bitcast.7, ...), custom_call_target="tpu_custom_call" | custom-call | flops 2113929216 | bytes 4128768 | tf_op jit(solution)/shard_map/expert_down/pallas_call | solution.py:431
  76.1 21.2 %write_results.1 = (bf16[384,384]{1,0:T(8,128)(2,1)}, bf16[336,256]{1,0:T(8,128)(2,1)}, bf16[336,256]{1,0:T(8,128)(2,1)}, f32[16,384]{1,0:T(8,128)}) custom-call(bf16[384,384]{1,0:T(8,128)(2,1)} %get-tuple-element.12.refs_0_, bf16[336,256]{1,0:T(8,128)(2,1)} %get-tuple-element.13.refs_1_, bf16[336,256]{1,0:T(8,128)(2,1)} %get-tuple-element.14.refs_2_, ...), custom_call_target="tpu_custom_call" | custom-call | tf_op jit(solution)/shard_map/write_results/pallas_call | solution.py:495

commit v3 on v2

--- a/solution.py
+++ b/solution.py
@@ -10,6 +10,8 @@
 BLOCK = 128
 MESH = pl.DeviceIdType.MESH
 RING = (1, 3, 2)
+NEXT = (1, 3)
+EARLY = 0
 F32 = jnp.float32
 BF16 = jnp.bfloat16
 
@@ -53,7 +55,11 @@
     nearb,
     farb,
     rgb,
+    gu,
+    gg,
+    comb,
     in_sem,
+    out_sem,
     ready,
     ag_ss,
     ag_rs,
@@ -109,16 +115,14 @@
     def greet(sem, d_dp, d_et):
         pl.semaphore_signal(sem, 1, device_id=(d_dp, d_et), device_id_type=MESH)
 
-    def greet_et(k, carry):
-        greet(barrier, dp, et_at(y + k // 4, x + k % 4))
-        return carry
-
     def line(k):
         return (((grp + ngrp + k) % ngrp) * 2 + zp) * 2 + c
 
+    for d in RING:
+        greet(barrier, dp, et_at(y, x + d))
+        greet(barrier, dp, et_at(y + d, x))
     greet(barrier, line(1), et)
     greet(barrier, line(-1), et)
-    lax.fori_loop(1, 16, greet_et, 0)
     for k in (1, 2, 3):
         greet(barrier, near_peer(k), et)
 
@@ -143,23 +147,29 @@
     loads["og"].wait()
     sg[et] = jnp.dot(onehot[...], og[...], preferred_element_type=F32).astype(BF16)
 
-    pl.semaphore_wait(barrier, 2 + 15 + 3)
+    pl.semaphore_wait(barrier, 6 + 2 + 3)
 
     sends = []
-
-    def send(block, h, d_et):
-        view = sg.at[block, pl.ds(h * half, half)]
-        cp = copy(view, view, ag_ss.at[len(sends)], ag_rs.at[block * 2 + h], dp, d_et)
+    quart = half // 2
+
+    def rows(block, h, q):
+        if q is None:
+            return sg.at[block, pl.ds(h * half, half)]
+        return sg.at[block, pl.ds(h * half + q * quart, quart)]
+
+    def send(block, h, d_et, q=None):
+        view = rows(block, h, q)
+        cp = copy(view, view, ag_ss.at[len(sends)], ag_rs.at[(block * 2 + h) * 2 + (q or 0)], dp, d_et)
         cp.start()
         sends.append(cp)
 
-    def wait_block(block, h):
-        arrived(sg.at[block, pl.ds(h * half, half)], ag_rs.at[block * 2 + h])
+    def wait_block(block, h, q=None):
+        arrived(rows(block, h, q), ag_rs.at[(block * 2 + h) * 2 + (q or 0)])
 
     for d in RING:
         send(et, 0, et_at(y, x + d))
         send(et, 1, et_at(y + d, x))
-    for d in RING:
+    for d in NEXT:
         send(et, 0, et_at(y + d, x))
         send(et, 1, et_at(y, x + d))
 
@@ -173,27 +183,28 @@
     hid_t[0:ff] = hidden
     hid[...] = hid_t[...].T.astype(BF16)
     wv[ff:ffp] = jnp.zeros((ffp - ff, wv.shape[1]), BF16)
-    loads["w"].wait()
 
     def forward_block(j, carry):
         w_j = wv[:, pl.ds(pl.multiple_of(j * cols, 128), cols)]
         part[j] = jnp.dot(hid[...], w_j, preferred_element_type=F32).astype(BF16)
         return carry
 
-    lax.fori_loop(0, 16, forward_block, 0)
-
-    ready_wait(0)
-    ready_signal(1)
-
-    for d in RING:
+    loads["w"].wait()
+    lax.fori_loop(0, 4, forward_block, 0)
+
+    for i, d in enumerate(RING):
         block = et_at(y, x + d)
         wait_block(block, 0)
-        for e in RING:
+        for e in NEXT:
             send(block, 0, et_at(y + e, x))
         block = et_at(y + d, x)
         wait_block(block, 1)
-        for e in RING:
+        for e in NEXT:
             send(block, 1, et_at(y, x + e))
+        lax.fori_loop(4 * i + 4, 4 * i + 8, forward_block, 0)
+
+    ready_wait(0)
+    ready_signal(1)
 
     loads["lg"].wait()
     logit = lg[...]
@@ -216,44 +227,19 @@
     loads["t"].wait()
     tslot[...] = jnp.dot(onehot[...], tv[...], preferred_element_type=F32).astype(BF16)
 
-    ready_wait(1)
-    ready_signal(2)
-
     def back(block):
         w_j = wv[0:ff, pl.ds(pl.multiple_of(block * cols, 128), cols)]
         return lax.dot_general(w_j, sg[block], (((1,), (1,)), ((), ())), preferred_element_type=F32)
 
-    raw[...] = back(et)
-    order = [(0, 1), (1, 0), (0, 3), (3, 0), (0, 2), (2, 0)]
-    order += [(1, 1), (1, 3), (3, 1), (3, 3), (1, 2), (2, 1), (3, 2), (2, 3), (2, 2)]
-    for dy, dx in order:
-        block = et_at(y + dy, x + dx)
-        if dx == 0:
-            wait_block(block, 0)
-        elif dy == 0:
-            wait_block(block, 1)
-        else:
-            wait_block(block, 0)
-            wait_block(block, 1)
-        raw[...] += back(block)
-
-    prod = hid_t[0:ff].astype(BF16).astype(F32) * raw[...]
-    wgb[et] = jnp.sum(prod, axis=0, keepdims=True)
-
-    def wg_copy(k):
-        return copy(wgb.at[et], wgb.at[et], wg_ss.at[k], wg_rs.at[et], dp, et_at(y + k // 4, x + k % 4))
-
-    def wg_send(k, carry):
-        wg_copy(k).start()
-        return carry
-
-    lax.fori_loop(1, 16, wg_send, 0)
+    def add_back(dy, dx):
+        raw[...] += back(et_at(y + dy, x + dx))
 
     first = []
-    for far_off in (2, 1, 3, 0):
-        for d in RING:
-            yy, xx = (y + far_off) % 4, (x + d) % 4
-            cp = copy(
+
+    def scatter(far_off, d):
+        yy, xx = (y + far_off) % 4, (x + d) % 4
+        first.append(
+            copy(
                 part.at[yy * 4 + xx, pl.ds(0, half)],
                 r1.at[0, x, yy],
                 r1_ss.at[len(first)],
@@ -261,10 +247,11 @@
                 dp,
                 et_at(y, xx),
             )
-            cp.start()
-            first.append(cp)
-            yy, xx = (y + d) % 4, (x + far_off) % 4
-            cp = copy(
+        )
+        first[-1].start()
+        yy, xx = (y + d) % 4, (x + far_off) % 4
+        first.append(
+            copy(
                 part.at[yy * 4 + xx, pl.ds(half, half)],
                 r1.at[1, y, xx],
                 r1_ss.at[len(first)],
@@ -272,14 +259,62 @@
                 dp,
                 et_at(yy, x),
             )
-            cp.start()
-            first.append(cp)
+        )
+        first[-1].start()
+
+    scatters = [(far_off, d) for far_off in (2, 1, 3, 0) for d in RING]
+
+    raw[...] = back(et)
+    whole = {0: [(1, 0), (3, 0), (0, 1), (0, 3)], 1: [(1, 1)], 3: [(1, 3), (3, 1), (3, 3)], 2: []}
+    for d in (0,) + RING:
+        for e in NEXT:
+            q = 1 if e == 1 else 0
+            block = et_at(y + e, x + d)
+            wait_block(block, 0)
+            send(block, 0, et_at(y + 4 - e, x), q)
+            block = et_at(y + d, x + e)
+            wait_block(block, 1)
+            send(block, 1, et_at(y, x + 4 - e), q)
+        for pair in whole[d]:
+            add_back(*pair)
+    ready_wait(1)
+    ready_signal(2)
+    for pair in scatters[:EARLY]:
+        scatter(*pair)
+    for d in (0,) + RING:
+        for q in (0, 1):
+            wait_block(et_at(y + 2, x + d), 0, q)
+            wait_block(et_at(y + d, x + 2), 1, q)
+        add_back(2, d)
+        if d != 2:
+            add_back(d, 2)
+
+    prod = hid_t[0:ff].astype(BF16).astype(F32) * raw[...]
+    wgb[et] = jnp.sum(prod, axis=0, keepdims=True)
+
+    def wg_copy(k):
+        return copy(wgb.at[et], wgb.at[et], wg_ss.at[k], wg_rs.at[et], dp, et_at(y + k // 4, x + k % 4))
+
+    def wg_send(k, carry):
+        wg_copy(k).start()
+        return carry
+
+    lax.fori_loop(1, 16, wg_send, 0)
+
+    for pair in scatters[EARLY:]:
+        scatter(*pair)
 
     gate = gt[...].astype(F32)
     sig = jax.nn.sigmoid(gate)
     back_p = ct[experts : experts + 1] * raw[...]
-    gu_ref[...] = (back_p * gate * sig).astype(BF16)
-    gg_ref[...] = (back_p * ut[...].astype(F32) * sig * (1.0 + gate * (1.0 - sig))).astype(BF16)
+    gu[...] = (back_p * gate * sig).astype(BF16)
+    gg[...] = (back_p * ut[...].astype(F32) * sig * (1.0 + gate * (1.0 - sig))).astype(BF16)
+    stores = [
+        pltpu.make_async_copy(gu, gu_ref, out_sem.at[0]),
+        pltpu.make_async_copy(gg, gg_ref, out_sem.at[1]),
+    ]
+    for cp in stores:
+        cp.start()
 
     def wg_wait(k, carry):
         src = et_at(y + k // 4, x + k % 4)
@@ -293,25 +328,30 @@
 
     lgrad = (ct[0:experts] * wg).astype(BF16)
     rpart = jnp.dot(lgrad, tslot[...], preferred_element_type=F32)
-    rp[0] = rpart[0:8]
-    rp[1] = rpart[8:16]
+    quarters = range(4)
+    chunks = range(cols // 128)
+    each = experts // 4
+    empty = jnp.zeros((rp.shape[1] - each * len(chunks), 128), F32)
+    for q in quarters:
+        own_rows = rpart[q * each : (q + 1) * each]
+        rp[q] = jnp.concatenate([own_rows[:, k * 128 : (k + 1) * 128] for k in chunks] + [empty], axis=0)
     mine = zp * 2 + c
     nears = []
+
+    def quarter_of(k):
+        return ((zp + k // 2) % 2) * 2 + (c + k) % 2
+
     for k in (1, 2, 3):
-        cp = copy(
-            rp.at[(c + k) % 2], nearb.at[mine], near_ss.at[k], near_rs.at[mine], near_peer(k), et
-        )
+        cp = copy(rp.at[quarter_of(k)], nearb.at[mine], near_ss.at[k], near_rs.at[mine], near_peer(k), et)
         cp.start()
         nears.append(cp)
-    nearb[mine] = rp[c]
+    nearb[mine] = rp[mine]
     for k in (1, 2, 3):
-        src = ((zp + k // 2) % 2) * 2 + (c + k) % 2
+        src = quarter_of(k)
         arrived(nearb.at[src], near_rs.at[src])
     total = ((nearb[0] + nearb[1]) + nearb[2]) + nearb[3]
 
-    pieces = [total[:, k * 128 : (k + 1) * 128] for k in range(cols // 128)]
-    pad = farb.shape[1] - 8 * len(pieces)
-    farb[grp] = jnp.concatenate(pieces + [jnp.zeros((pad, 128), F32)], axis=0).astype(BF16)
+    farb[grp] = total.astype(BF16)
 
     def far_copy(k):
         return copy(farb.at[grp], farb.at[grp], far_ss.at[k], far_rs.at[grp], line(k), et)
@@ -360,9 +400,13 @@
         return acc + farb[k].astype(F32)
 
     total = lax.fori_loop(1, ngrp, far_add, farb[0].astype(F32)) * scale
-    rgb[c] = jnp.concatenate([total[k * 8 : (k + 1) * 8] for k in range(cols // 128)], axis=1)
-    swap = copy(rgb.at[c], rgb.at[c], core_ss, core_rs, near_peer(1), et)
-    swap.start()
+    rgb[...] = total
+    for k in (1, 2, 3):
+        cp = copy(rgb, rg_ref.at[mine], core_ss.at[k], core_rs.at[mine], near_peer(k), et)
+        cp.start()
+        nears.append(cp)
+    stores.append(pltpu.make_async_copy(rgb, rg_ref.at[mine], out_sem.at[2]))
+    stores[-1].start()
 
     out_rows = []
     for h in (0, 1):
@@ -375,13 +419,17 @@
         out_rows.append(
             (acc * pm[h * half : (h + 1) * half, 0:1]).astype(BF16)
         )
-    comb_ref[...] = lax.dot_general(
+    comb[...] = lax.dot_general(
         onehot[...], jnp.concatenate(out_rows, axis=0), (((0,), (0,)), ((), ())), preferred_element_type=F32
     ).astype(BF16)
 
-    arrived(rgb.at[1 - c], core_rs)
-    rg_ref[0:8] = rgb[0]
-    rg_ref[8:16] = rgb[1]
+    stores.append(pltpu.make_async_copy(comb, comb_ref, out_sem.at[3]))
+    stores[-1].start()
+    for k in (1, 2, 3):
+        src = quarter_of(k)
+        arrived(rg_ref.at[src], core_rs.at[src])
+    for cp in stores:
+        cp.wait()
 
     for cp in sends + first + second + nears:
         cp.wait_send()
@@ -396,16 +444,25 @@
 
     lax.fori_loop(1, 16, wg_done, 0)
     lax.fori_loop(1, ngrp, far_done, 0)
-    swap.wait_send()
-
-
-def finish(*refs):
-    n = len(refs) // 2
-    sems = refs[-1]
-    copies = [pltpu.make_async_copy(refs[i], refs[n + i], sems.at[i]) for i in range(n)]
-    for cp in copies:
+
+
+def finish(n, *refs):
+    held, rows, in_sem, out_sem = refs[2 * n : 3 * n], refs[3 * n], refs[3 * n + 1], refs[3 * n + 2]
+    ins = [pltpu.make_async_copy(refs[i], held[i], in_sem.at[i]) for i in range(n)]
+    outs = [pltpu.make_async_copy(held[i] if i < n - 1 else rows, refs[n + i], out_sem.at[i]) for i in range(n)]
+    for cp in ins:
         cp.start()
-    for cp in copies:
+    for cp, out in zip(ins[:-1], outs[:-1]):
+        cp.wait()
+        out.start()
+    ins[-1].wait()
+    each = rows.shape[0] // 4
+    for q in range(4):
+        for k in range(rows.shape[1] // 128):
+            piece = held[-1][q, k * each : (k + 1) * each]
+            rows[q * each : (q + 1) * each, k * 128 : (k + 1) * 128] = piece
+    outs[-1].start()
+    for cp in outs:
         cp.wait()
 
 
@@ -417,22 +474,21 @@
     wide = down_weight.shape[1]
     ngrp = nz // 2
     experts = router_logits.shape[1]
-    far_rows = -(-(8 * (cols // 128)) // 16) * 16
+    far_rows = -(-(experts // 4 * (cols // 128)) // 16) * 16
     scale = float((toks * nz * 2) ** -0.5)
-    vmem = pl.BlockSpec(memory_space=pltpu.VMEM)
     hbm = pl.BlockSpec(memory_space=pltpu.HBM)
     dma = pltpu.SemaphoreType.DMA
     shapes = (
         jax.ShapeDtypeStruct((toks, cols), BF16),
         jax.ShapeDtypeStruct((ff, slots), BF16),
         jax.ShapeDtypeStruct((ff, slots), BF16),
-        jax.ShapeDtypeStruct((experts, cols), F32),
+        jax.ShapeDtypeStruct((4, far_rows, 128), F32),
     )
     results = pl.pallas_call(
         functools.partial(kernel, nz, scale),
         out_shape=shapes,
         in_specs=[hbm, pl.BlockSpec(memory_space=pltpu.SMEM), hbm, hbm, hbm, hbm, hbm, hbm],
-        out_specs=(vmem, vmem, vmem, vmem),
+        out_specs=(hbm,) * len(shapes),
         scratch_shapes=[
             pltpu.VMEM((1, slots), jnp.int32),
             pltpu.VMEM((experts, toks), F32),
@@ -454,14 +510,18 @@
             pltpu.VMEM((2, 4, half, cols), BF16),
             pltpu.VMEM((2, 4, half, cols), BF16),
             pltpu.VMEM((16, 1, slots), F32),
-            pltpu.VMEM((2, 8, cols), F32),
-            pltpu.VMEM((4, 8, cols), F32),
+            pltpu.VMEM((4, far_rows, 128), F32),
+            pltpu.VMEM((4, far_rows, 128), F32),
             pltpu.VMEM((ngrp, far_rows, 128), BF16),
-            pltpu.VMEM((2, 8, cols), F32),
+            pltpu.VMEM((far_rows, 128), F32),
+            pltpu.VMEM((ff, slots), BF16),
+            pltpu.VMEM((ff, slots), BF16),
+            pltpu.VMEM((toks, cols), BF16),
             dma((7,)),
+            dma((4,)),
             pltpu.SemaphoreType.REGULAR((8,)),
-            dma((30,)),
-            dma((32,)),
+            dma((38,)),
+            dma((64,)),
             dma((24,)),
             dma((32,)),
             dma((8,)),
@@ -472,8 +532,8 @@
             dma((4,)),
             dma((ngrp,)),
             dma((ngrp,)),
-            dma,
-            dma,
+            dma((4,)),
+            dma((4,)),
         ],
         compiler_params=pltpu.CompilerParams(
             collective_id=1, has_side_effects=True, vmem_limit_bytes=62 * 2**20
@@ -493,11 +553,12 @@
         out_grad,
     )
     combined, grad_gate, grad_up, router_grad = pl.pallas_call(
-        finish,
-        out_shape=shapes,
+        functools.partial(finish, len(shapes)),
+        out_shape=shapes[:-1] + (jax.ShapeDtypeStruct((experts, cols), F32),),
         in_specs=[hbm] * len(shapes),
         out_specs=(hbm,) * len(shapes),
-        scratch_shapes=[dma((len(shapes),))],
+        scratch_shapes=[pltpu.VMEM(a.shape, a.dtype) for a in shapes]
+        + [pltpu.VMEM((experts, cols), F32), dma((len(shapes),)), dma((len(shapes),))],
         compiler_params=pltpu.CompilerParams(vmem_limit_bytes=62 * 2**20),
         name="write_results",
     )(*results)

time: 98.1 us -> 71.6 us (0.73)
  Pallas kernels: 96.1 us -> 70.2 us
    pallas_call x1, Pallas kernels: 21.2 us -> 1.86 us  [body(): pl.pallas_call(functools.partial(finish, len(shapes)), out_shape=shapes[:...]
    pallas_call x1, Pallas kernels: 74.8 us -> 68.3 us  [body(): pl.pallas_call(functools.partial(kernel, nz, scale), out_shape=shapes, in...]
where the time goes in v3:
time: 71.6 us; the launch traced here: 71.5 us
  Pallas kernels  70.2 us (98%)
  between operations  1.29 us (2%)
    pallas_call x1, Pallas kernels, body(): pl.pallas_call(functools.partial(kernel, nz, scale), out_shape=shapes, in...  68.3 us
    pallas_call x1, Pallas kernels, body(): pl.pallas_call(functools.partial(finish, len(shapes)), out_shape=shapes[:...  1.86 us

profile of v3, /device:TPU:1, one launch (start us, length us, event | category | flops | bytes accessed | tf_op | source)
XLA Modules:
  0.0 71.5 jit_solution(9425756164304958456)
XLA Ops:
  1.3 68.3 %expert_down.1 = (bf16[384,384]{1,0:T(8,128)(2,1)}, bf16[336,256]{1,0:T(8,128)(2,1)}, bf16[336,256]{1,0:T(8,128)(2,1)}, f32[4,16,128]{2,1,0:T(8,128)}) custom-call(s32[1,256]{1,0:T(1,128)} %bitcast.11, s32[1]{0:T(128)S(6)} %copy.12.bc_ref, f32[16,384]{1,0:T(8,128)} %bitcast.10, bf16[336,256]{1,0:T(8,128)(2,1)} %bitcast.6, bf16[336,256]{1,0:T(8,128)(2,1)} %bitcast.7, ...), custom_call_target="tpu_custom_call" | custom-call | flops 2113929216 | bytes 4128768 | tf_op jit(solution)/shard_map/expert_down/pallas_call | solution.py:487
  69.6 1.9 %write_results.1 = (bf16[384,384]{1,0:T(8,128)(2,1)}, bf16[336,256]{1,0:T(8,128)(2,1)}, bf16[336,256]{1,0:T(8,128)(2,1)}, f32[16,384]{1,0:T(8,128)}) custom-call(bf16[384,384]{1,0:T(8,128)(2,1)} %get-tuple-element.12.refs_0_, bf16[336,256]{1,0:T(8,128)(2,1)} %get-tuple-element.13.refs_1_, bf16[336,256]{1,0:T(8,128)(2,1)} %get-tuple-element.14.refs_2_, ...), custom_call_target="tpu_custom_call" | custom-call | tf_op jit(solution)/shard_map/write_results/pallas_call | solution.py:555
